TPU v7x, 512 devices: a whole 4x8x8 slice. The times are simulated.
512 devices in a mesh: seq: 32 (over x, z), tp: 8 (over y), dp: 2 (over core).
Axes of the slice: x: 4, y: 8, z: 8, core: 2. Of those that a mesh axis runs over, the one named last changes fastest.
Arguments:
- qkv_bank: bfloat16 [32768, 3, 4096], P(('dp', 'seq'), None, 'tp'), parts along dimension 0, may hold values from -6 to 6
- pack_rows: int32 [256], P(('dp', 'seq')), parts along dimension 0, may hold values from 0 to 127, as said below
- segment: int32 [256], P(('dp', 'seq')), parts along dimension 0, may hold values from 0 to 7, never falling along the last dimension, each value on 1 to 64 neighbouring positions
- norm_gain: float32 [4096], P('tp'), may hold values from 0.1 to 1.9
- out_weight: bfloat16 [4096, 4096], P('seq', 'tp'), may hold values from -0.09375 to 0.09375
Outputs:
- mixed: bfloat16 [32768, 4096], P(('dp', 'seq'), 'tp'), parts along dimension 0
There are 2 independent parts, one for each index of `dp`. A program takes and returns all parts, laid end to end along the dimension named above; an argument that names none is the same for every part. Nothing has to cross between parts.
Inputs may be any that keep to these rules, and one draw needn't show every extreme that they name: Packed block t takes block pack_rows[t]; the 4 packed blocks of each aligned group of 4 take the same group's 4 source blocks in some order. Segment ids never fall along the packed blocks; a segment covers at most 64 blocks, and one covers exactly that many.
All inputs are finite; a program needn't handle non-finite values.
Results may differ from a plain program's by a relative error of at most 0.0057.
Values may be sent and summed in bfloat16 or wider, within the bound.
A program may use at most 64 MiB of HBM per device.

v0:
```python
import jax
import jax.numpy as jnp
from jax import lax
from jax.sharding import PartitionSpec as P

DH = 128
BLK = 128


def prefix_2(value, axis, join, neutral):
    count, mine = (lax.axis_size(axis), lax.axis_index(axis))
    pieces = jax.tree.map(lambda part: lax.all_gather(part, axis), value)
    total = jax.tree.map(
        lambda part, zero: jnp.full_like(part, 0) + jnp.asarray(zero, part.dtype), value, neutral
    )

    def hop(position, total):
        longer = join(total, jax.tree.map(lambda part: part[position], pieces))
        return jax.tree.map(lambda new, old: jnp.where(position < mine, new, old), longer, total)

    return lax.fori_loop(0, count - 1, hop, total)


def combine(earlier, later):
    e_state, e_first, e_last = earlier
    l_state, l_first, l_last = later
    joins = (l_first == l_last) & (e_last == l_first)
    state = jnp.where(l_last < 0, e_state, l_state + jnp.where(joins, e_state, 0.0))
    first = jnp.where(e_last < 0, l_first, e_first)
    last = jnp.where(l_last < 0, e_last, l_last)
    return (state, first, last)


def body(qkv_bank, pack_rows, segment, norm_gain, out_weight):
    row_count = qkv_bank.shape[0]
    blocks_here = row_count // BLK
    heads_here = qkv_bank.shape[2] // DH
    position = lax.axis_index("seq")
    local_ids = pack_rows - position * blocks_here
    blocks = qkv_bank.reshape(blocks_here, BLK, 3, heads_here, DH)
    packed = jnp.take(blocks, local_ids, axis=0)
    queries = packed[:, :, 0]
    keys = packed[:, :, 1]
    values = packed[:, :, 2]
    updates = jnp.einsum("bjhd,bjhe->bhde", keys, values, preferred_element_type=jnp.float32)
    seg_float = segment.astype(jnp.float32)
    same_seg = seg_float[:, None] == seg_float[None, :]
    block_ids = jnp.arange(blocks_here)
    earlier_mask = (same_seg & (block_ids[:, None] > block_ids[None, :])).astype(jnp.float32)
    local_prefix = jnp.einsum(
        "bc,chde->bhde", earlier_mask, updates, precision=lax.Precision.HIGHEST
    )
    tail_mask = same_seg[blocks_here - 1].astype(jnp.float32)
    summary = jnp.einsum("c,chde->hde", tail_mask, updates, precision=lax.Precision.HIGHEST)
    first_seg = seg_float[0]
    last_seg = seg_float[blocks_here - 1]
    empty = (jnp.zeros_like(summary), jnp.float32(-1.0), jnp.float32(-1.0))
    in_state, in_first, in_last = prefix_2((summary, first_seg, last_seg), "seq", combine, empty)
    carried = (seg_float == in_last).astype(jnp.float32)
    prefix = (local_prefix + carried[:, None, None, None] * in_state[None]).astype(jnp.bfloat16)
    inter = jnp.einsum("bihd,bhde->bihe", queries, prefix, preferred_element_type=jnp.float32)
    scores = jnp.einsum("bihd,bjhd->bhij", queries, keys, preferred_element_type=jnp.float32)
    causal = jnp.arange(BLK)[:, None] >= jnp.arange(BLK)[None, :]
    scores = jnp.where(causal[None, None], scores, 0.0).astype(jnp.bfloat16)
    intra = jnp.einsum("bhij,bjhe->bihe", scores, values, preferred_element_type=jnp.float32)
    attended = inter + intra
    scale = lax.rsqrt(jnp.mean(attended * attended, axis=-1, keepdims=True) + 1e-06)
    gains = norm_gain.reshape(heads_here, DH)
    normed = (attended * scale * gains[None, None]).astype(jnp.bfloat16)
    normed = normed.reshape(row_count, heads_here * DH)
    features = lax.all_gather(normed, "tp", axis=1, tiled=True)
    mixed = jnp.dot(
        features,
        lax.all_gather(out_weight, "seq", axis=0, tiled=True),
        preferred_element_type=jnp.float32,
    )
    return mixed.astype(jnp.bfloat16)


def solution(mesh):
    in_specs = (
        P(("dp", "seq"), None, "tp"),
        P(("dp", "seq")),
        P(("dp", "seq")),
        P("tp"),
        P("seq", "tp"),
    )
    out_specs = P(("dp", "seq"), "tp")
    return jax.shard_map(body, mesh=mesh, in_specs=in_specs, out_specs=out_specs, check_vma=False)
```

profile of v0, /device:TPU:6, one launch (start us, length us, event | category | flops | bytes accessed | tf_op | source)
XLA Modules:
  0.0 370.7 jit_solution(9160218823506157888)
XLA Ops:
  6.5 0.7 compare_and_fusion
  7.2 2.4 reshape.36
  10.0 1.9 gather_fusion
  11.9 1.6 copy_select_fusion
  14.2 2.4 fusion.3
  16.7 0.7 all-gather.7.cloned.1.call-update
  17.5 1.2 dynamic-slice
  18.7 0.6 slice_dynamic-update-slice_fusion
  19.4 0.7 slice_dynamic-update-slice_fusion.1
  20.1 69.8 %all-reduce.2 = (f32[32]{0:T(128)S(1)}, f32[32]{0:T(128)S(1)}) all-reduce(f32[32]{0:T(128)S(1)} %slice_dynamic-update-slice_fusion.1, f32[32]{0:T(128)S(1)} %slice_dynamic-update-slice_fusion), channel_id=1, replica_groups=mesh['seq'=32,'tp'=8,'dp'=2] {'seq'}, use_global_device_ids=true, to_apply=%add | all-reduce | flops 64 | bytes 512
  89.8 34.5 %all-gather.9.cloned.1.call-done = f32[128,128,128]{2,1,0:T(8,128)} async-done(((f32[4,128,128]{2,1,0:T(8,128)}), f32[128,128,128]{2,1,0:T(8,128)}) %all-gather.9.cloned.1.call-update) | async-done | bytes 8388624 | tf_op jit(solution)/shard_map/all_gather | solution.py:12
  124.3 170.8 %while.16 = (s32[]{:T(128)}, f32[4,128,128]{2,1,0:T(8,128)S(1)}, f32[]{:T(128)}, s32[]{:T(128)}, f32[32]{0:T(128)S(1)}, /*index=5*/f32[32,4,128,128]{3,2,1,0:T(8...) while((s32[]{:T(128)}, f32[4,128,128]{2,1,0:T(8,128)S(1)}, f32[]{:T(128)}, s32[]{:T(128)}, ...), condition=%wide.region_1.2_spmd.clone, body=%wide.region_0.1_spmd.clone.sunk | while | flops 327690 | bytes 786639 | solution.py:21
  128.1 1.1 select_select_fusion.2
  133.6 1.1 select_select_fusion.2
  139.1 1.1 select_select_fusion.2
  144.6 1.1 select_select_fusion.2
  150.1 1.1 select_select_fusion.2
  151.9 0.6 dynamic_slice.30
  155.6 1.1 select_select_fusion.2
  157.4 0.6 dynamic_slice.30
  161.1 1.1 select_select_fusion.2
  162.9 0.6 dynamic_slice.30
  166.6 1.1 select_select_fusion.2
  168.4 0.6 dynamic_slice.30
  172.2 1.1 select_select_fusion.2
  177.7 1.1 select_select_fusion.2
  183.2 1.1 select_select_fusion.2
  184.9 0.6 dynamic_slice.30
  188.7 1.1 select_select_fusion.2
  190.4 0.6 dynamic_slice.30
  194.2 1.1 select_select_fusion.2
  199.7 1.1 select_select_fusion.2
  201.5 0.6 dynamic_slice.30
  205.2 1.1 select_select_fusion.2
  207.0 0.6 dynamic_slice.30
  210.7 1.1 select_select_fusion.2
  212.5 0.6 dynamic_slice.30
  216.3 1.1 select_select_fusion.2
  218.0 0.6 dynamic_slice.30
  221.8 1.1 select_select_fusion.2
  223.5 0.6 dynamic_slice.30
  227.3 1.1 select_select_fusion.2
  232.8 1.1 select_select_fusion.2
  238.3 1.1 select_select_fusion.2
  243.8 1.1 select_select_fusion.2
  249.3 1.1 select_select_fusion.2
  254.8 1.1 select_select_fusion.2
  260.3 1.1 select_select_fusion.2
  265.8 1.1 select_select_fusion.2
  271.3 1.1 select_select_fusion.2
  273.1 0.6 dynamic_slice.30
  276.8 1.1 select_select_fusion.2
  278.6 0.6 dynamic_slice.30
  282.4 1.1 select_select_fusion.2
  284.1 0.6 dynamic_slice.30
  287.9 1.1 select_select_fusion.2
  289.6 0.6 dynamic_slice.30
  293.4 1.1 select_select_fusion.2
  295.1 1.8 fusion.1
  296.9 1.5 fusion.6
  298.4 2.1 multiply_reduce_fusion
  301.1 0.9 copy.42
  302.0 55.6 %all-gather.5.cloned.1.call-done = bf16[512,4096]{1,0:T(8,128)(2,1)} async-done(((bf16[512,512]{1,0:T(8,128)(2,1)}), bf16[512,4096]{1,0:T(8,128)(2,1)}) %all-gather.5.cloned.1.call-update) | async-done | bytes 4194320 | tf_op jit(solution)/shard_map/all_gather | solution.py:71
  357.6 6.6 %convolution_convert_fusion = bf16[512,512]{1,0:T(8,128)(2,1)} fusion(bf16[512,4096]{1,0:T(8,128)(2,1)} %all-gather.5.cloned.1.call-done, bf16[4096,512]{1,0:T(8,128)(2,1)} %all-gather.7.cloned.1.call-done), kind=kOutput, calls=%fused_computation.9 | convolution fusion | flops 2147745792 | bytes 8912896 | tf_op jit(solution)/shard_map/dot_general | solution.py:72
  (70 shorter events, 29.6 us)
Async XLA Ops:
  6.5 117.8 %all-gather.9.cloned.1.call-start = ((), (), s32[]{:S(2)}) async-start(), calls=%async_computation.2 | async-start | bytes 8650752 | tf_op jit(solution)/shard_map/all_gather | solution.py:12
  13.5 0.7 copy-start.1
  16.6 285.3 %all-gather.7.cloned.1.call-start = ((), (), s32[]{:S(2)}) async-start(), calls=%async_computation.1 | async-start | bytes 4325376 | tf_op jit(solution)/shard_map/all_gather | solution.py:74
  17.4 340.2 %all-gather.5.cloned.1.call-start = ((), (), s32[]{:S(2)}) async-start(), calls=%async_computation | async-start | bytes 4718592 | tf_op jit(solution)/shard_map/all_gather | solution.py:71
  298.4 2.1 copy-start
Sparse Core Ops, SparseCore 0:
  16.8 107.5 all-gather.8
  127.5 84.9 all-gather.6
  302.1 55.4 all-gather.4
where the time goes:
time: 374 us; the launch traced here: 371 us
  loops' own time  100 us (27%)
  waiting for transfers between devices  90.8 us (24%)
  blocking collectives  69.8 us (19%)
  local copies, waits for them, and re-layouts  45.8 us (12%)
  other arithmetic  35.9 us (10%)
  matrix products  14.7 us (4%)
  between operations  13.2 us (4%)
    another operation x1, loops' own time, prefix_2(): return lax.fori_loop(0, count - 1, hop, total)  100 us
    unnamed x1, blocking collectives  69.8 us
    all_gather x1, waiting for transfers between devices, body(): features = lax.all_gather(normed, 'tp', axis=1, tiled=True)  55.6 us
    dynamic_slice x62, local copies, waits for them, and re-layouts, hop(): longer = join(total, jax.tree.map(lambda part: part[position], pieces))  37 us
    all_gather x1, waiting for transfers between devices, prefix_2(): pieces = jax.tree.map(lambda part: lax.all_gather(part, axis), value)  34.5 us
    select_n x31, other arithmetic, hop(): jnp.where(position < mine, new, old)  33.4 us
  transfers between devices with their start and end apart: 3, of which 2 were waited for; matrix products, arithmetic and copies ran while one was open for 22% of the time, Pallas kernels for 0%

commit v1 on v0

v1 whole, which is shorter than its diff:
```python
import jax
import jax.numpy as jnp
from jax import lax
from jax.experimental import pallas as pl
from jax.experimental.pallas import tpu as pltpu
from jax.sharding import PartitionSpec as P

DH = 128
BLK = 128
NB = 4
NH = 4
NX, NZ, NY = 4, 8, 8
PIECE = NH * DH // NZ
W0 = 48
MESH = pl.DeviceIdType.MESH
F32, BF16 = jnp.float32, jnp.bfloat16


def dot(a, b, dims=(((1,), (0,)), ((), ()))):
    return lax.dot_general(a, b, dims, preferred_element_type=F32)


def same(a, b):
    return jnp.maximum(1 - jnp.abs(a - b), 0).astype(F32)


def hops(direction, block):
    return 4 if (block < NB // 2) == (direction == 0) else 3


def kernel(
    pack_ref, seg_ref, qkv_hbm, gain_ref, w_hbm, out_ref,
    qbuf, kbuf, vbuf, wbuf, feats, acc, intra, local, tsend, pieces, infos, ascan, rbuf, csend, carry,
    load_sem, info_s, info_r, t_s, t_r, r_s, r_r, c_s, c_r,
    y_s, y_r, wx_s, wx_r, wz_s, wz_r, pair_s, pair_r,
):
    seq, tp, core = lax.axis_index("seq"), lax.axis_index("tp"), lax.axis_index("dp")
    x, z = seq // NZ, seq % NZ

    def at_z(step):
        return {"seq": x * NZ + (z + step) % NZ, "tp": tp, "dp": core}

    def at_x(step):
        return {"seq": (x + step) % NX * NZ + z, "tp": tp, "dp": core}

    def at_y(step):
        return {"seq": seq, "tp": (tp + step) % NY, "dp": core}

    sibling = {"seq": seq, "tp": tp, "dp": 1 - core}

    def remote(src, dst, send, recv, device):
        return pltpu.make_async_remote_copy(
            src_ref=src, dst_ref=dst, send_sem=send, recv_sem=recv,
            device_id=device, device_id_type=MESH,
        )

    loads = [pltpu.make_async_copy(qkv_hbm.at[p], to, load_sem.at[p]) for p, to in enumerate((qbuf, kbuf, vbuf))]
    rows_of = (pl.ds(0, W0), pl.ds(W0, BLK - W0))
    w_load = [
        pltpu.make_async_copy(w_hbm.at[rows], wbuf.at[x, z, rows], load_sem.at[3]) for rows in rows_of
    ]

    for p in (1, 2, 0):
        loads[p].start()
    for c in range(2):
        pl.when(core == c)(w_load[c].start)
    partners = [at_z(i) for i in range(1, NZ)] + [at_x(i) for i in range(1, NX)]
    partners += [at_y(1), at_y(NY - 1), sibling]
    barrier = pltpu.get_barrier_semaphore()
    for device in partners:
        pl.semaphore_signal(barrier, inc=1, device_id=device, device_id_type=MESH)
    segs = [seg_ref[b] for b in range(NB)]
    infos[z, 0:4, :] = jnp.broadcast_to(segs[0], (4, DH)).astype(F32)
    infos[z, 4:8, :] = jnp.broadcast_to(segs[NB - 1], (4, DH)).astype(F32)
    pl.semaphore_wait(barrier, len(partners))

    info_copies = [
        remote(infos.at[z], infos.at[z], info_s.at[i - 1], info_r.at[i - 1], at_z(i))
        for i in range(1, NZ)
    ]
    for copy in info_copies:
        copy.start()

    w_x0 = [
        remote(wbuf.at[x, z, rows_of[0]], wbuf.at[x, z, rows_of[0]], wx_s.at[i - 1], wx_r.at[i - 1], at_x(i))
        for i in range(1, NX)
    ]
    w_z0 = [
        remote(wbuf.at[:, z, rows_of[0]], wbuf.at[:, z, rows_of[0]], wz_s.at[i - 1], wz_r.at[i - 1], at_z(i))
        for i in range(1, NZ)
    ]
    w_z1 = [
        remote(wbuf.at[x, z, rows_of[1]], wbuf.at[x, z, rows_of[1]], wz_s.at[i - 1], wz_r.at[i - 1], at_z(i))
        for i in range(1, NZ)
    ]
    w_x1 = [
        remote(wbuf.at[x, :, rows_of[1]], wbuf.at[x, :, rows_of[1]], wx_s.at[i - 1], wx_r.at[i - 1], at_x(i))
        for i in range(1, NX)
    ]

    @pl.when(core == 0)
    def _():
        w_load[0].wait()
        for copy in w_x0:
            copy.start()

    @pl.when(core == 1)
    def _():
        w_load[1].wait()

    ids = [lax.rem(pack_ref[b], NB) for b in range(NB)]
    heads = [pl.ds(h * DH, DH) for h in range(NH)]
    joins = [None] + [same(segs[b], segs[b - 1]) for b in range(1, NB)]
    loads[1].wait()
    loads[2].wait()
    for h in range(NH):
        total = None
        for b in range(NB):
            key = kbuf[ids[b], :, heads[h]]
            value = vbuf[ids[b], :, heads[h]]
            update = dot(key, value, (((0,), (0,)), ((), ())))
            if b > 0:
                before = total * joins[b]
                local[b - 1, h] = before
                total = before + update
            else:
                total = update
        tsend[pl.ds(h * DH, DH), :] = total.astype(BF16)

    def piece(j):
        return pl.ds(pl.multiple_of(j * PIECE, PIECE), PIECE)

    t_copies = [
        remote(tsend.at[piece((z + i) % NZ)], pieces.at[z], t_s.at[i - 1], t_r.at[i - 1], at_z(i))
        for i in range(1, NZ)
    ]
    for copy in t_copies:
        copy.start()
    pieces[z] = tsend[piece(z), :]

    loads[0].wait()
    causal = lax.broadcasted_iota(jnp.int32, (BLK, BLK), 0) >= lax.broadcasted_iota(jnp.int32, (BLK, BLK), 1)

    def block_rows(b):
        return pl.ds(b * BLK, BLK)

    for b in range(NB):
        for h in range(NH):
            query = qbuf[ids[b], :, heads[h]]
            key = kbuf[ids[b], :, heads[h]]
            value = vbuf[ids[b], :, heads[h]]
            score = dot(query, key, (((1,), (1,)), ((), ())))
            score = jnp.where(causal, score, 0.0).astype(BF16)
            intra[block_rows(b), heads[h]] = dot(score, value)

    for copy in info_copies:
        copy.wait_recv()
    for copy in t_copies:
        copy.wait_recv()
    firsts = [infos[j, 0:1, :] for j in range(NZ)]
    lasts = [infos[j, 4:5, :] for j in range(NZ)]
    running = None
    for j in range(NZ):
        part = pieces[j].astype(F32)
        if j > 0:
            before = same(firsts[j], lasts[j - 1]) * running
            ascan[j] = before
            running = part + same(firsts[j], lasts[j]) * before
        else:
            running = part
    rbuf[x, 0:PIECE, :] = running
    rbuf[x, PIECE:PIECE + 8, :] = jnp.broadcast_to(lasts[NZ - 1], (8, DH))
    r_copies = [
        remote(rbuf.at[x], rbuf.at[x], r_s.at[i - 1], r_r.at[i - 1], at_x(i)) for i in range(1, NX)
    ]
    for copy in r_copies:
        copy.start()
    for copy in r_copies:
        copy.wait_recv()
    for j in range(NZ):
        into = ascan[j] if j > 0 else jnp.zeros((PIECE, DH), F32)
        for xx in range(NX - 1):
            hit = same(rbuf[xx, PIECE:PIECE + 1, :], firsts[j]) * jnp.where(xx < x, 1.0, 0.0)
            into = into + hit * rbuf[xx, 0:PIECE, :]
        csend[j] = into.astype(BF16)
    c_copies = [
        remote(csend.at[(z + i) % NZ], carry.at[z], c_s.at[i - 1], c_r.at[i - 1], at_z(i))
        for i in range(1, NZ)
    ]
    for copy in c_copies:
        copy.start()
    carry[z] = csend[z]

    @pl.when(core == 0)
    def _():
        for copy in w_x0:
            copy.wait_recv()
        for copy in w_z0:
            copy.start()

    @pl.when(core == 1)
    def _():
        for copy in w_z1:
            copy.start()

    for copy in c_copies:
        copy.wait_recv()

    def y_copy(direction, step, b):
        source = (tp - step) % NY if direction == 0 else (tp + step) % NY
        ref = feats.at[source, block_rows(b)]
        to = at_y(1) if direction == 0 else at_y(NY - 1)
        return remote(ref, ref, y_s.at[direction, step, b], y_r.at[direction, step, b], to)

    gains = gain_ref[...]
    for b in range(NB):
        carried = same(segs[b], segs[0])
        for h in range(NH):
            state = carry[pl.ds(h * 2, 2)].reshape(DH, DH).astype(F32) * carried
            if b > 0:
                state = state + local[b - 1, h]
            query = qbuf[ids[b], :, heads[h]]
            attended = intra[block_rows(b), heads[h]] + dot(query, state.astype(BF16))
            scale = lax.rsqrt(jnp.mean(attended * attended, axis=-1, keepdims=True) + 1e-06)
            normed = attended * scale * gains[:, h * DH:(h + 1) * DH]
            feats[tp, block_rows(b), heads[h]] = normed.astype(BF16)
        for direction in range(2):
            y_copy(direction, 0, b).start()

    def arrive(step, b):
        for direction in range(2):
            if hops(direction, b) > step:
                y_copy(direction, step, b).wait_recv()
                if hops(direction, b) > step + 1:
                    y_copy(direction, step + 1, b).start()

    for b in range(NB - 1):
        arrive(0, b)

    @pl.when(core == 1)
    def _():
        for copy in w_z1:
            copy.wait_recv()
        for copy in w_x1:
            copy.start()

    arrive(0, NB - 1)
    for b in range(NB):
        arrive(1, b)

    pair = [remote(wbuf.at[:, :, rows], wbuf.at[:, :, rows], pair_s, pair_r, sibling) for rows in rows_of]

    @pl.when(core == 0)
    def _():
        for copy in w_z0:
            copy.wait_recv()
        pair[0].start()

    @pl.when(core == 1)
    def _():
        for copy in w_x1:
            copy.wait_recv()
        pair[1].start()

    for b in range(NB):
        arrive(2, b)
    for c in range(2):
        pl.when(core == c)(pair[1 - c].wait_recv)

    def weights(source):
        return wbuf[source // 2, pl.ds(source % 2 * NH, NH)].reshape(NH * DH, NH * DH)

    acc[...] = dot(feats[tp], weights(tp))

    def product(i, _):
        source = (tp + jnp.where(i < 3, i + 1, i + 2)) % NY
        acc[...] += dot(feats[source], weights(source))
        return 0

    lax.fori_loop(0, NY - 2, product, 0)

    far = (tp + NY // 2) % NY
    for b in (0, NB // 2, 1, NB // 2 + 1):
        arrive(3, b)
        mixed = acc[block_rows(b), :] + dot(feats[far, block_rows(b), :], weights(far))
        out_ref[block_rows(b), :] = mixed.astype(BF16)

    for copy in info_copies + t_copies + r_copies + c_copies:
        copy.wait_send()
    for direction in range(2):
        for b in range(NB):
            for step in range(hops(direction, b)):
                y_copy(direction, step, b).wait_send()

    @pl.when(core == 0)
    def _():
        for copy in w_x0 + w_z0:
            copy.wait_send()
        pair[0].wait_send()

    @pl.when(core == 1)
    def _():
        for copy in w_z1 + w_x1:
            copy.wait_send()
        pair[1].wait_send()


def body(qkv_bank, pack_rows, segment, norm_gain, out_weight):
    rows, _, columns = qkv_bank.shape
    planes = jnp.transpose(qkv_bank, (1, 0, 2)).reshape(3, NB, BLK, columns)
    dma = pltpu.SemaphoreType.DMA
    return pl.pallas_call(
        kernel,
        out_shape=jax.ShapeDtypeStruct((rows, columns), BF16),
        in_specs=[
            pl.BlockSpec(memory_space=pltpu.SMEM),
            pl.BlockSpec(memory_space=pltpu.SMEM),
            pl.BlockSpec(memory_space=pl.ANY),
            pl.BlockSpec(memory_space=pltpu.VMEM),
            pl.BlockSpec(memory_space=pl.ANY),
        ],
        out_specs=pl.BlockSpec(memory_space=pltpu.VMEM),
        scratch_shapes=[
            pltpu.VMEM((NB, BLK, columns), BF16),
            pltpu.VMEM((NB, BLK, columns), BF16),
            pltpu.VMEM((NB, BLK, columns), BF16),
            pltpu.VMEM((NX, NZ, BLK, columns), BF16),
            pltpu.VMEM((NY, rows, columns), BF16),
            pltpu.VMEM((rows, columns), F32),
            pltpu.VMEM((rows, columns), F32),
            pltpu.VMEM((NB - 1, NH, DH, DH), F32),
            pltpu.VMEM((NH * DH, DH), BF16),
            pltpu.VMEM((NZ, PIECE, DH), BF16),
            pltpu.VMEM((NZ, 8, DH), F32),
            pltpu.VMEM((NZ, PIECE, DH), F32),
            pltpu.VMEM((NX, PIECE + 8, DH), F32),
            pltpu.VMEM((NZ, PIECE, DH), BF16),
            pltpu.VMEM((NZ, PIECE, DH), BF16),
            dma((4,)),
            dma((NZ - 1,)), dma((NZ - 1,)), dma((NZ - 1,)), dma((NZ - 1,)),
            dma((NX - 1,)), dma((NX - 1,)), dma((NZ - 1,)), dma((NZ - 1,)),
            dma((2, 4, NB)), dma((2, 4, NB)),
            dma((NX - 1,)), dma((NX - 1,)), dma((NZ - 1,)), dma((NZ - 1,)),
            dma, dma,
        ],
        compiler_params=pltpu.CompilerParams(
            collective_id=0, has_side_effects=True, vmem_limit_bytes=48 * 1024 * 1024
        ),
    )(pack_rows, segment, planes, norm_gain.reshape(1, columns), out_weight)


def solution(mesh):
    in_specs = (
        P(("dp", "seq"), None, "tp"),
        P(("dp", "seq")),
        P(("dp", "seq")),
        P("tp"),
        P("seq", "tp"),
    )
    out_specs = P(("dp", "seq"), "tp")
    return jax.shard_map(body, mesh=mesh, in_specs=in_specs, out_specs=out_specs, check_vma=False)
```

time: 374 us -> 77.2 us (0.21)
  the two profiles are of different devices: /device:TPU:6 before, /device:TPU:8 now
where the time goes in v1:
time: 77.2 us; the launch traced here: 77 us
  Pallas kernels  71.9 us (93%)
  local copies, waits for them, and re-layouts  5.1 us (7%)
    pallas_call x1, Pallas kernels, body(): pl.pallas_call(kernel, out_shape=jax.ShapeDtypeStruct((rows, columns), BF...  71.9 us
    unnamed x11, local copies, waits for them, and re-layouts  5.1 us

profile of v1, /device:TPU:8, one launch (start us, length us, event | category | flops | bytes accessed | tf_op | source)
XLA Modules:
  0.0 77.0 jit_solution(814136853801957531)
XLA Ops:
  0.0 0.0 copy-start
  0.0 1.4 %copy-done = bf16[512,3,512]{2,0,1:T(8,128)(2,1)S(1)} copy-done((bf16[512,3,512]{2,0,1:T(8,128)(2,1)S(1)}, bf16[512,3,512]{2,0,1:T(8,128)(2,1)}, u32[]{:S(2)}) %copy-start) | copy-done | bytes 1572888
  1.4 0.0 copy-start.1
  1.4 0.9 %copy-done.1 = bf16[128,512]{1,0:T(8,128)(2,1)S(1)} copy-done((bf16[128,512]{1,0:T(8,128)(2,1)S(1)}, bf16[128,512]{1,0:T(8,128)(2,1)}, u32[]{:S(2)}) %copy-start.1) | copy-done | bytes 131096
  2.3 0.0 copy-start.2
  2.3 0.7 copy-done.2
  3.0 0.0 copy-start.3
  3.0 0.7 copy-done.3
  3.7 0.0 copy-start.4
  3.7 0.7 copy-done.4
  4.3 71.9 %shard_map.55 = bf16[512,512]{1,0:T(8,128)(2,1)S(1)} custom-call(s32[4]{0:T(128)S(1)} %copy-done.3, s32[4]{0:T(128)S(1)} %copy-done.4, bf16[3,4,128,512]{3,2,1,0:T(8,128)(2,1)S(1)} %bitcast.4, f32[1,512]{1,0:T(1,128)S(1)} %bitcast.5, bf16[128,512]{1,0:T(8,128)(2,1)S(1)} %copy-done.1), custom_call_target="tpu_custom_call" | custom-call | tf_op jit(solution)/shard_map/pallas_call | solution.py:312
  76.2 0.8 %copy.7 = bf16[512,512]{1,0:T(8,128)(2,1)} copy(bf16[512,512]{1,0:T(8,128)(2,1)S(1)} %shard_map.55) | data formatting | bytes 1048576
Async XLA Ops:
  0.0 1.4 %copy-start = (bf16[512,3,512]{2,0,1:T(8,128)(2,1)S(1)}, bf16[512,3,512]{2,0,1:T(8,128)(2,1)}, u32[]{:S(2)}) copy-start(bf16[512,3,512]{2,0,1:T(8,128)(2,1)} %param.5) | copy-start | bytes 4718596
  1.4 0.9 %copy-start.1 = (bf16[128,512]{1,0:T(8,128)(2,1)S(1)}, bf16[128,512]{1,0:T(8,128)(2,1)}, u32[]{:S(2)}) copy-start(bf16[128,512]{1,0:T(8,128)(2,1)} %w_hbm.1) | copy-start | bytes 393220
  2.3 0.7 copy-start.2
  3.0 0.7 copy-start.3
  3.7 0.7 copy-start.4

commit v2 on v0

v2 whole, which is shorter than its diff:
```python
import jax
import jax.numpy as jnp
from jax import lax
from jax.experimental import pallas as pl
from jax.experimental.pallas import tpu as pltpu
from jax.sharding import PartitionSpec as P

DH = 128
BLK = 128
NB = 4
NH = 4
NG = 2
GH = NH // NG
GC = GH * DH
NX, NZ, NY = 4, 8, 8
PIECE = GC // NZ
HALF = BLK // 2
MESH = pl.DeviceIdType.MESH
F32, BF16 = jnp.float32, jnp.bfloat16


def dot(a, b, dims=(((1,), (0,)), ((), ()))):
    return lax.dot_general(a, b, dims, preferred_element_type=F32)


def same(a, b):
    return jnp.maximum(1 - jnp.abs(a - b), 0).astype(F32)


def hops(direction, part):
    return 4 if (part < 2) == (direction == 0) else 3


def kernel(
    pack_ref, seg_ref, qkv_hbm, gain_ref, w_hbm, out_hbm,
    qbuf, kbuf, vbuf, wbuf, feats, acc, intra, local, tsend, pieces, infos, ascan, rbuf, csend, carry, mixed,
    load_sem, out_sem, info_s, info_r, t_s, t_r, r_s, r_r, c_s, c_r,
    y_s, y_r, wx_s, wx_r, wz_s, wz_r, own_s, own_r, pair_s, pair_r,
):
    seq, tp, core = lax.axis_index("seq"), lax.axis_index("tp"), lax.axis_index("dp")
    x, z = seq // NZ, seq % NZ

    def at_z(step):
        return {"seq": x * NZ + (z + step) % NZ, "tp": tp, "dp": core}

    def at_x(step):
        return {"seq": (x + step) % NX * NZ + z, "tp": tp, "dp": core}

    def at_y(step):
        return {"seq": seq, "tp": (tp + step) % NY, "dp": core}

    sibling = {"seq": seq, "tp": tp, "dp": 1 - core}

    def remote(src, dst, send, recv, device):
        return pltpu.make_async_remote_copy(
            src_ref=src, dst_ref=dst, send_sem=send, recv_sem=recv,
            device_id=device, device_id_type=MESH,
        )

    loads = [
        pltpu.make_async_copy(qkv_hbm.at[p], to, load_sem.at[p]) for p, to in enumerate((qbuf, kbuf, vbuf))
    ]
    w_load = pltpu.make_async_copy(w_hbm.at[core], wbuf.at[x, z, core], load_sem.at[3])
    loads[1].start()
    loads[2].start()
    partners = [at_z(i) for i in (4, 3, 5, 2, 6, 1, 7)] + [at_x(i) for i in (2, 1, 3)]
    partners += [at_y(1), at_y(NY - 1), sibling]
    barrier = pltpu.get_barrier_semaphore()
    for device in partners:
        pl.semaphore_signal(barrier, inc=1, device_id=device, device_id_type=MESH)
    loads[0].start()
    w_load.start()
    segs = [seg_ref[b] for b in range(NB)]
    infos[z, 0:4, :] = jnp.broadcast_to(segs[0], (4, DH)).astype(F32)
    infos[z, 4:8, :] = jnp.broadcast_to(segs[NB - 1], (4, DH)).astype(F32)

    ids = [lax.rem(pack_ref[b], NB) for b in range(NB)]
    heads = [pl.ds(h * DH, DH) for h in range(NH)]
    joins = [None] + [same(segs[b], segs[b - 1]) for b in range(1, NB)]

    def update(g):
        for h in range(GH):
            head = g * GH + h
            total = None
            for b in range(NB):
                key = kbuf[ids[b], :, heads[head]]
                value = vbuf[ids[b], :, heads[head]]
                new = dot(key, value, (((0,), (0,)), ((), ())))
                if b > 0:
                    before = total * joins[b]
                    local[b - 1, head] = before
                    total = before + new
                else:
                    total = new
            tsend[g, pl.ds(h * DH, DH), :] = total.astype(BF16)
        pieces[g, z] = tsend[g, piece(z), :]

    def piece(j):
        return pl.ds(pl.multiple_of(j * PIECE, PIECE), PIECE)

    far_first = (4, 3, 5, 2, 6, 1, 7)
    info_copies = [
        remote(infos.at[z], infos.at[z], info_s.at[i - 1], info_r.at[i - 1], at_z(i)) for i in far_first
    ]
    t_copies = [
        [
            remote(tsend.at[g, piece((z + i) % NZ)], pieces.at[g, z], t_s.at[g, i - 1], t_r.at[g, i - 1], at_z(i))
            for i in far_first
        ]
        for g in range(NG)
    ]
    w_x = [
        remote(wbuf.at[x, z, core], wbuf.at[x, z, core], wx_s.at[i - 1], wx_r.at[i - 1], at_x(i)) for i in (2, 1, 3)
    ]
    loads[1].wait()
    loads[2].wait()
    update(0)
    pl.semaphore_wait(barrier, len(partners))
    for copy in t_copies[0] + info_copies:
        copy.start()
    update(1)
    for copy in t_copies[1]:
        copy.start()
    w_load.wait()
    for copy in w_x:
        copy.start()

    loads[0].wait()
    causal = lax.broadcasted_iota(jnp.int32, (BLK, BLK), 0) >= lax.broadcasted_iota(jnp.int32, (BLK, BLK), 1)

    def block_rows(b):
        return pl.ds(b * BLK, BLK)

    for h in range(NH):
        for b in range(NB):
            query = qbuf[ids[b], :, heads[h]]
            key = kbuf[ids[b], :, heads[h]]
            value = vbuf[ids[b], :, heads[h]]
            score = dot(query, key, (((1,), (1,)), ((), ())))
            score = jnp.where(causal, score, 0.0).astype(BF16)
            intra[block_rows(b), heads[h]] = dot(score, value)

    for copy in info_copies:
        copy.wait_recv()
    firsts = [infos[j, 0:1, :] for j in range(NZ)]
    lasts = [infos[j, 4:5, :] for j in range(NZ)]
    stays = [same(firsts[j], lasts[j]) for j in range(NZ)]
    follows = [None] + [same(firsts[j], lasts[j - 1]) for j in range(1, NZ)]
    r_copies = [
        [remote(rbuf.at[g, x], rbuf.at[g, x], r_s.at[g, i - 1], r_r.at[g, i - 1], at_x(i)) for i in (2, 1, 3)]
        for g in range(NG)
    ]
    c_copies = [
        [
            remote(csend.at[g, (z + i) % NZ], carry.at[g, z], c_s.at[g, i - 1], c_r.at[g, i - 1], at_z(i))
            for i in far_first
        ]
        for g in range(NG)
    ]
    for g in range(NG):
        for copy in t_copies[g]:
            copy.wait_recv()
        running = pieces[g, 0].astype(F32)
        for j in range(1, NZ):
            before = follows[j] * running
            ascan[g, j] = before
            running = pieces[g, j].astype(F32) + stays[j] * before
        rbuf[g, x, 0:PIECE, :] = running
        rbuf[g, x, PIECE:PIECE + 8, :] = jnp.broadcast_to(lasts[NZ - 1], (8, DH))
        for copy in r_copies[g]:
            copy.start()
    for g in range(NG):
        for copy in r_copies[g]:
            copy.wait_recv()
        for j in range(NZ):
            into = ascan[g, j] if j > 0 else jnp.zeros((PIECE, DH), F32)
            for xx in range(NX - 1):
                hit = same(rbuf[g, xx, PIECE:PIECE + 1, :], firsts[j]) * jnp.where(xx < x, 1.0, 0.0)
                into = into + hit * rbuf[g, xx, 0:PIECE, :]
            csend[g, j] = into.astype(BF16)
        for copy in c_copies[g]:
            copy.start()
        carry[g, z] = csend[g, z]

    def w_copy(direction, step, j):
        source = (z - step) % NZ if direction == 0 else (z + step) % NZ
        ref = wbuf.at[j, source, core]
        to = at_z(1) if direction == 0 else at_z(NZ - 1)
        return remote(ref, ref, wz_s.at[direction, step, j], wz_r.at[direction, step, j], to)

    def w_pair(direction, step, j):
        source = (z - 1 - step) % NZ if direction == 0 else (z + 1 + step) % NZ
        ref = wbuf.at[j, source, core]
        return remote(ref, ref, pair_s.at[direction, step, j], pair_r.at[direction, step, j], sibling)

    own_pair = remote(wbuf.at[:, z, core], wbuf.at[:, z, core], own_s, own_r, sibling)
    for copy in w_x:
        copy.wait_recv()
    for j in range(NX):
        for direction in range(2):
            w_copy(direction, 0, j).start()
    own_pair.start()

    def w_arrive(step, j):
        for direction in range(2):
            if hops(direction, j) > step:
                w_copy(direction, step, j).wait_recv()
                if hops(direction, j) > step + 1:
                    w_copy(direction, step + 1, j).start()
                w_pair(direction, step, j).start()

    def y_copy(direction, step, g, b):
        source = (tp - step) % NY if direction == 0 else (tp + step) % NY
        ref = feats.at[source, g, block_rows(b)]
        to = at_y(1) if direction == 0 else at_y(NY - 1)
        return remote(ref, ref, y_s.at[direction, step, g, b], y_r.at[direction, step, g, b], to)

    def y_arrive(step, g, b):
        for direction in range(2):
            if hops(direction, b) > step:
                y_copy(direction, step, g, b).wait_recv()
                if hops(direction, b) > step + 1:
                    y_copy(direction, step + 1, g, b).start()

    gains = gain_ref[...]
    for g in range(NG):
        for copy in c_copies[g]:
            copy.wait_recv()
        for b in range(NB):
            carried = same(segs[b], segs[0])
            for h in range(GH):
                head = g * GH + h
                state = carry[g, pl.ds(h * NZ // GH, NZ // GH)].reshape(DH, DH).astype(F32) * carried
                if b > 0:
                    state = state + local[b - 1, head]
                query = qbuf[ids[b], :, heads[head]]
                attended = intra[block_rows(b), heads[head]] + dot(query, state.astype(BF16))
                scale = lax.rsqrt(jnp.mean(attended * attended, axis=-1, keepdims=True) + 1e-06)
                normed = attended * scale * gains[:, head * DH:(head + 1) * DH]
                feats[tp, g, block_rows(b), heads[h]] = normed.astype(BF16)
            for direction in range(2):
                y_copy(direction, 0, g, b).start()

    def weights(source, g):
        return wbuf[source // 2, pl.ds(source % 2 * NH + g * GH, GH)].reshape(GC, NH * DH)

    def product(step):
        source = (tp + step) % NY
        total = dot(feats[source, 0], weights(source, 0)) + dot(feats[source, 1], weights(source, 1))
        acc[...] = total if step == 0 else acc[...] + total

    parts = [(g, b) for g in range(NG) for b in range(NB)]
    w_order = [(step, j) for step in range(4) for j in range(NX)]
    for step in range(2):
        for i, (g, b) in enumerate(parts):
            y_arrive(step, g, b)
            w_arrive(*w_order[step * len(parts) + i])
    own_pair.wait_recv()
    for step, j in w_order:
        for direction in range(2):
            if hops(direction, j) > step:
                w_pair(direction, step, j).wait_recv()
    for i, (g, b) in enumerate(parts):
        y_arrive(2, g, b)
        if i < 5:
            product((0, 1, NY - 1, 2, NY - 2)[i])
    product(3)
    product(NY - 3)

    far = (tp + NY // 2) % NY
    out_copies = []
    for b in (0, NB // 2, 1, NB // 2 + 1):
        y_arrive(3, 0, b)
        y_arrive(3, 1, b)
        rows = block_rows(b)
        last = dot(feats[far, 0, rows, :], weights(far, 0)) + dot(feats[far, 1, rows, :], weights(far, 1))
        mixed[rows, :] = (acc[rows, :] + last).astype(BF16)
        out_copies.append(pltpu.make_async_copy(mixed.at[rows], out_hbm.at[rows], out_sem.at[b]))
        out_copies[-1].start()

    for copy in info_copies + w_x + [own_pair]:
        copy.wait_send()
    for g in range(NG):
        for copy in t_copies[g] + r_copies[g] + c_copies[g]:
            copy.wait_send()
    for direction in range(2):
        for part in range(4):
            for step in range(hops(direction, part)):
                w_copy(direction, step, part).wait_send()
                w_pair(direction, step, part).wait_send()
                for g in range(NG):
                    y_copy(direction, step, g, part).wait_send()
    for copy in out_copies:
        copy.wait()


def body(qkv_bank, pack_rows, segment, norm_gain, out_weight):
    rows, _, columns = qkv_bank.shape
    planes = jnp.transpose(qkv_bank, (1, 0, 2)).reshape(3, NB, BLK, columns)
    dma = pltpu.SemaphoreType.DMA
    return pl.pallas_call(
        kernel,
        out_shape=jax.ShapeDtypeStruct((rows, columns), BF16),
        in_specs=[
            pl.BlockSpec(memory_space=pltpu.SMEM),
            pl.BlockSpec(memory_space=pltpu.SMEM),
            pl.BlockSpec(memory_space=pl.ANY),
            pl.BlockSpec(memory_space=pltpu.VMEM),
            pl.BlockSpec(memory_space=pl.ANY),
        ],
        out_specs=pl.BlockSpec(memory_space=pl.ANY),
        scratch_shapes=[
            pltpu.VMEM((NB, BLK, columns), BF16),
            pltpu.VMEM((NB, BLK, columns), BF16),
            pltpu.VMEM((NB, BLK, columns), BF16),
            pltpu.VMEM((NX, NZ, 2, HALF, columns), BF16),
            pltpu.VMEM((NY, NG, rows, GC), BF16),
            pltpu.VMEM((rows, columns), F32),
            pltpu.VMEM((rows, columns), F32),
            pltpu.VMEM((NB - 1, NH, DH, DH), F32),
            pltpu.VMEM((NG, GC, DH), BF16),
            pltpu.VMEM((NG, NZ, PIECE, DH), BF16),
            pltpu.VMEM((NZ, 8, DH), F32),
            pltpu.VMEM((NG, NZ, PIECE, DH), F32),
            pltpu.VMEM((NG, NX, PIECE + 8, DH), F32),
            pltpu.VMEM((NG, NZ, PIECE, DH), BF16),
            pltpu.VMEM((NG, NZ, PIECE, DH), BF16),
            pltpu.VMEM((rows, columns), BF16),
            dma((4,)), dma((NB,)),
            dma((NZ - 1,)), dma((NZ - 1,)), dma((NG, NZ - 1)), dma((NG, NZ - 1)),
            dma((NG, NX - 1)), dma((NG, NX - 1)), dma((NG, NZ - 1)), dma((NG, NZ - 1)),
            dma((2, 4, NG, NB)), dma((2, 4, NG, NB)),
            dma((NX - 1,)), dma((NX - 1,)), dma((2, 4, NX)), dma((2, 4, NX)),
            dma, dma, dma((2, 4, NX)), dma((2, 4, NX)),
        ],
        compiler_params=pltpu.CompilerParams(
            collective_id=0, has_side_effects=True, vmem_limit_bytes=60 * 1024 * 1024
        ),
    )(pack_rows, segment, planes, norm_gain.reshape(1, columns), out_weight.reshape(2, HALF, columns))


def solution(mesh):
    in_specs = (
        P(("dp", "seq"), None, "tp"),
        P(("dp", "seq")),
        P(("dp", "seq")),
        P("tp"),
        P("seq", "tp"),
    )
    out_specs = P(("dp", "seq"), "tp")
    return jax.shard_map(body, mesh=mesh, in_specs=in_specs, out_specs=out_specs, check_vma=False)
```

time: 374 us -> 73.7 us (0.20)
  the two profiles are of different devices: /device:TPU:6 before, /device:TPU:16 now
where the time goes in v2:
time: 73.7 us; the launch traced here: 73.5 us
  Pallas kernels  71.6 us (97%)
  local copies, waits for them, and re-layouts  1.87 us (3%)
    pallas_call x1, Pallas kernels, body(): pl.pallas_call(kernel, out_shape=jax.ShapeDtypeStruct((rows, columns), BF...  71.6 us
    unnamed x1, local copies, waits for them, and re-layouts  1.87 us

profile of v2, /device:TPU:16, one launch (start us, length us, event | category | flops | bytes accessed | tf_op | source)
XLA Modules:
  0.0 73.5 jit_solution(12406857186937686572)
XLA Ops:
  0.0 71.6 %shard_map.55 = bf16[512,512]{1,0:T(8,128)(2,1)} custom-call(s32[4]{0:T(128)} %pack_ref.1, s32[4]{0:T(128)} %seg_ref.1, bf16[3,4,128,512]{3,2,1,0:T(8,128)(2,1)} %bitcast.5, f32[1,512]{1,0:T(1,128)} %bitcast.7, bf16[2,64,512]{2,1,0:T(8,128)(2,1)} %bitcast.6), custom_call_target="tpu_custom_call" | custom-call | tf_op jit(solution)/shard_map/pallas_call | solution.py:301
  71.6 1.9 %copy.7 = bf16[512,512]{1,0:T(8,128)(2,1)} copy(bf16[512,512]{1,0:T(8,128)(2,1)} %shard_map.55) | data formatting | bytes 1048576

commit v3 on v2

v3 whole, which is shorter than its diff:
```python
import jax
import jax.numpy as jnp
from jax import lax
from jax.experimental import pallas as pl
from jax.experimental.pallas import tpu as pltpu
from jax.sharding import PartitionSpec as P

DH = 128
BLK = 128
NB = 4
NH = 4
NG = 2
GH = NH // NG
GC = GH * DH
NX, NZ, NY = 4, 8, 8
PIECE = GC // NZ
HALF = BLK // 2
MESH = pl.DeviceIdType.MESH
F32, BF16 = jnp.float32, jnp.bfloat16


def dot(a, b, dims=(((1,), (0,)), ((), ()))):
    return lax.dot_general(a, b, dims, preferred_element_type=F32)


def same(a, b):
    return jnp.maximum(1 - jnp.abs(a - b), 0).astype(F32)


def hops(direction, part):
    return 4 if (part < 2) == (direction == 0) else 3


def kernel(
    pack_hbm, seg_hbm, qkv_hbm, gain_hbm, w_hbm, out_ref,
    pack_ref, seg_ref, gain_ref, qbuf, kbuf, vbuf, wbuf, feats, acc, intra, local, tsend, pieces, infos, ascan, rbuf,
    csend, carry,
    load_sem, info_s, info_r, t_s, t_r, r_s, r_r, c_s, c_r,
    y_s, y_r, wx_s, wx_r, wz_s, wz_r, pair_s, pair_r,
):
    seq, tp, core = lax.axis_index("seq"), lax.axis_index("tp"), lax.axis_index("dp")
    x, z = seq // NZ, seq % NZ

    def at_z(step):
        return {"seq": x * NZ + (z + step) % NZ, "tp": tp, "dp": core}

    def at_x(step):
        return {"seq": (x + step) % NX * NZ + z, "tp": tp, "dp": core}

    def at_y(step):
        return {"seq": seq, "tp": (tp + step) % NY, "dp": core}

    sibling = {"seq": seq, "tp": tp, "dp": 1 - core}

    def remote(src, dst, send, recv, device):
        return pltpu.make_async_remote_copy(
            src_ref=src, dst_ref=dst, send_sem=send, recv_sem=recv,
            device_id=device, device_id_type=MESH,
        )

    def wait_all(ref, sem):
        pltpu.make_async_copy(ref, ref, sem).wait()

    loads = [
        pltpu.make_async_copy(src, dst, load_sem.at[i])
        for i, (src, dst) in enumerate((
            (qkv_hbm.at[0], qbuf), (qkv_hbm.at[1], kbuf), (qkv_hbm.at[2], vbuf), (w_hbm.at[core], wbuf.at[x, z, core]),
            (pack_hbm, pack_ref), (seg_hbm, seg_ref), (gain_hbm, gain_ref),
        ))
    ]
    for i in (5, 4, 1, 2, 0, 3, 6):
        loads[i].start()
    partners = [at_z(i) for i in (4, 3, 5, 2, 6, 1, 7)] + [at_x(i) for i in (2, 1, 3)]
    partners += [at_y(1), at_y(NY - 1), sibling]
    barrier = pltpu.get_barrier_semaphore()
    for device in partners:
        pl.semaphore_signal(barrier, inc=1, device_id=device, device_id_type=MESH)
    loads[5].wait()
    loads[4].wait()
    segs = [seg_ref[b] for b in range(NB)]
    infos[z, 0:1, :] = jnp.broadcast_to(segs[0], (1, DH)).astype(F32)
    infos[z, 1:2, :] = jnp.broadcast_to(segs[NB - 1], (1, DH)).astype(F32)

    ids = [lax.rem(pack_ref[b], NB) for b in range(NB)]
    heads = [pl.ds(h * DH, DH) for h in range(NH)]
    joins = [None] + [same(segs[b], segs[b - 1]) for b in range(1, NB)]

    def update(g):
        for h in range(GH):
            head = g * GH + h
            total = None
            for b in range(NB):
                key = kbuf[ids[b], :, heads[head]]
                value = vbuf[ids[b], :, heads[head]]
                new = dot(key, value, (((0,), (0,)), ((), ())))
                if b > 0:
                    before = total * joins[b]
                    local[b - 1, head] = before
                    total = before + new
                else:
                    total = new
            tsend[g, pl.ds(h * DH, DH), :] = total.astype(BF16)
        pieces[g, z] = tsend[g, piece(z), :]

    def piece(j):
        return pl.ds(pl.multiple_of(j * PIECE, PIECE), PIECE)

    far_first = (4, 3, 5, 2, 6, 1, 7)
    def send_tails(g):
        for i in far_first:
            remote(tsend.at[g, piece((z + i) % NZ)], pieces.at[g, z], t_s, t_r.at[g], at_z(i)).start()

    loads[1].wait()
    loads[2].wait()
    update(0)
    pl.semaphore_wait(barrier, len(partners))
    send_tails(0)
    for i in far_first:
        remote(infos.at[z], infos.at[z], info_s, info_r, at_z(i)).start()
    update(1)
    send_tails(1)
    loads[3].wait()
    for i in (2, 1, 3):
        remote(wbuf.at[x, z, core], wbuf.at[x, z, core], wx_s, wx_r, at_x(i)).start()

    loads[0].wait()
    causal = lax.broadcasted_iota(jnp.int32, (BLK, BLK), 0) >= lax.broadcasted_iota(jnp.int32, (BLK, BLK), 1)

    def block_rows(b):
        return pl.ds(b * BLK, BLK)

    for h in range(NH):
        for b in range(NB):
            query = qbuf[ids[b], :, heads[h]]
            key = kbuf[ids[b], :, heads[h]]
            value = vbuf[ids[b], :, heads[h]]
            score = dot(query, key, (((1,), (1,)), ((), ())))
            score = jnp.where(causal, score, 0.0).astype(BF16)
            intra[block_rows(b), heads[h]] = dot(score, value)

    wait_all(infos.at[pl.ds(0, NZ - 1)], info_r)
    firsts = [infos[j, 0:1, :] for j in range(NZ)]
    lasts = [infos[j, 1:2, :] for j in range(NZ)]
    stays = [same(firsts[j], lasts[j]) for j in range(NZ)]
    follows = [None] + [same(firsts[j], lasts[j - 1]) for j in range(1, NZ)]
    for g in range(NG):
        wait_all(pieces.at[g, pl.ds(0, NZ - 1)], t_r.at[g])
        running = pieces[g, 0].astype(F32)
        for j in range(1, NZ):
            before = follows[j] * running
            ascan[g, j] = before
            running = pieces[g, j].astype(F32) + stays[j] * before
        rbuf[g, x, 0:PIECE, :] = running
        rbuf[g, x, PIECE:PIECE + 8, :] = jnp.broadcast_to(lasts[NZ - 1], (8, DH))
        for i in (2, 1, 3):
            remote(rbuf.at[g, x], rbuf.at[g, x], r_s, r_r.at[g], at_x(i)).start()
    for g in range(NG):
        wait_all(rbuf.at[g, pl.ds(0, NX - 1)], r_r.at[g])
        for j in range(NZ):
            into = ascan[g, j] if j > 0 else jnp.zeros((PIECE, DH), F32)
            for xx in range(NX - 1):
                hit = same(rbuf[g, xx, PIECE:PIECE + 1, :], firsts[j]) * jnp.where(xx < x, 1.0, 0.0)
                into = into + hit * rbuf[g, xx, 0:PIECE, :]
            csend[g, j] = into.astype(BF16)
        for i in far_first:
            remote(csend.at[g, (z + i) % NZ], carry.at[g, z], c_s, c_r.at[g], at_z(i)).start()
        carry[g, z] = csend[g, z]

    def w_ref(part, column, side):
        return wbuf.at[pl.ds(2 * part, 2), column, side]

    def w_copy(direction, step, part):
        source = (z - step) % NZ if direction == 0 else (z + step) % NZ
        ref = w_ref(part, source, core)
        to = at_z(1) if direction == 0 else at_z(NZ - 1)
        return remote(ref, ref, wz_s, wz_r.at[direction, step, part], to)

    def w_pair(ref):
        return remote(ref, ref, pair_s, pair_r, sibling)

    wait_all(wbuf.at[pl.ds(0, NX - 1), z, core], wx_r)
    for part in range(2):
        for direction in range(2):
            w_copy(direction, 0, part).start()
    w_pair(wbuf.at[:, z, core]).start()

    def w_arrive(step, part):
        for direction in range(2):
            if hops(direction, 2 * part) > step:
                w_copy(direction, step, part).wait_recv()
                if hops(direction, 2 * part) > step + 1:
                    w_copy(direction, step + 1, part).start()
                source = (z - 1 - step) % NZ if direction == 0 else (z + 1 + step) % NZ
                w_pair(w_ref(part, source, core)).start()

    def y_copy(direction, step, g, b):
        source = (tp - step) % NY if direction == 0 else (tp + step) % NY
        ref = feats.at[source, g, block_rows(b)]
        to = at_y(1) if direction == 0 else at_y(NY - 1)
        return remote(ref, ref, y_s, y_r.at[direction, step, g, b], to)

    def y_arrive(step, g, b):
        for direction in range(2):
            if hops(direction, b) > step:
                y_copy(direction, step, g, b).wait_recv()
                if hops(direction, b) > step + 1:
                    y_copy(direction, step + 1, g, b).start()

    loads[6].wait()
    gains = gain_ref[...]
    for g in range(NG):
        wait_all(carry.at[g, pl.ds(0, NZ - 1)], c_r.at[g])
        for b in range(NB):
            carried = same(segs[b], segs[0])
            for h in range(GH):
                head = g * GH + h
                state = carry[g, pl.ds(h * NZ // GH, NZ // GH)].reshape(DH, DH).astype(F32) * carried
                if b > 0:
                    state = state + local[b - 1, head]
                query = qbuf[ids[b], :, heads[head]]
                attended = intra[block_rows(b), heads[head]] + dot(query, state.astype(BF16))
                scale = lax.rsqrt(jnp.mean(attended * attended, axis=-1, keepdims=True) + 1e-06)
                normed = attended * scale * gains[:, head * DH:(head + 1) * DH]
                feats[tp, g, block_rows(b), heads[h]] = normed.astype(BF16)
            for direction in range(2):
                y_copy(direction, 0, g, b).start()

    def weights(source, g):
        return wbuf[source // 2, pl.ds(source % 2 * NH + g * GH, GH)].reshape(GC, NH * DH)

    def product(step):
        source = (tp + step) % NY
        total = dot(feats[source, 0], weights(source, 0)) + dot(feats[source, 1], weights(source, 1))
        acc[...] = total if step == 0 else acc[...] + total

    parts = [(g, b) for g in range(NG) for b in range(NB)]
    w_order = [(step, part) for step in range(4) for part in range(2)]
    for step in range(2):
        for i, (g, b) in enumerate(parts):
            y_arrive(step, g, b)
            if i % 2 == 1:
                w_arrive(*w_order[step * NB + i // 2])
    wait_all(wbuf.at[:, :, 1 - core], pair_r)
    for i, (g, b) in enumerate(parts):
        y_arrive(2, g, b)
        if i < 5:
            product((0, 1, NY - 1, 2, NY - 2)[i])
    product(3)
    product(NY - 3)

    far = (tp + NY // 2) % NY
    for g in range(NG):
        for b in (0, NB // 2, 1, NB // 2 + 1):
            y_arrive(3, g, b)
            rows = block_rows(b)
            total = acc[rows, :] + dot(feats[far, g, rows, :], weights(far, g))
            if g < NG - 1:
                acc[rows, :] = total
            else:
                out_ref[rows, :] = total.astype(BF16)

    wait_all(infos.at[pl.ds(0, NZ - 1)], info_s)
    wait_all(pieces.at[:, pl.ds(0, NZ - 1)], t_s)
    wait_all(rbuf.at[:, pl.ds(0, NX - 1)], r_s)
    wait_all(carry.at[:, pl.ds(0, NZ - 1)], c_s)
    wait_all(wbuf.at[pl.ds(0, NX - 1), z, core], wx_s)
    wait_all(wbuf.at[:, pl.ds(0, NZ - 1), core], wz_s)
    wait_all(wbuf.at[:, :, core], pair_s)
    wait_all(feats.at[pl.ds(0, NY - 1)], y_s)


def body(qkv_bank, pack_rows, segment, norm_gain, out_weight):
    rows, _, columns = qkv_bank.shape
    planes = jnp.transpose(qkv_bank, (1, 0, 2)).reshape(3, NB, BLK, columns)
    dma = pltpu.SemaphoreType.DMA
    return pl.pallas_call(
        kernel,
        out_shape=jax.ShapeDtypeStruct((rows, columns), BF16),
        in_specs=[pl.BlockSpec(memory_space=pl.ANY)] * 5,
        out_specs=pl.BlockSpec(memory_space=pltpu.VMEM),
        scratch_shapes=[
            pltpu.SMEM((NB,), jnp.int32),
            pltpu.SMEM((NB,), jnp.int32),
            pltpu.VMEM((1, columns), F32),
            pltpu.VMEM((NB, BLK, columns), BF16),
            pltpu.VMEM((NB, BLK, columns), BF16),
            pltpu.VMEM((NB, BLK, columns), BF16),
            pltpu.VMEM((NX, NZ, 2, HALF, columns), BF16),
            pltpu.VMEM((NY, NG, rows, GC), BF16),
            pltpu.VMEM((rows, columns), F32),
            pltpu.VMEM((rows, columns), F32),
            pltpu.VMEM((NB - 1, NH, DH, DH), F32),
            pltpu.VMEM((NG, GC, DH), BF16),
            pltpu.VMEM((NG, NZ, PIECE, DH), BF16),
            pltpu.VMEM((NZ, 2, DH), F32),
            pltpu.VMEM((NG, NZ, PIECE, DH), F32),
            pltpu.VMEM((NG, NX, PIECE + 8, DH), F32),
            pltpu.VMEM((NG, NZ, PIECE, DH), BF16),
            pltpu.VMEM((NG, NZ, PIECE, DH), BF16),
            dma((7,)), dma, dma, dma, dma((NG,)), dma, dma((NG,)), dma, dma((NG,)),
            dma, dma((2, 4, NG, NB)), dma, dma, dma, dma((2, 4, 2)), dma, dma,
        ],
        compiler_params=pltpu.CompilerParams(
            collective_id=0, has_side_effects=True, vmem_limit_bytes=60 * 1024 * 1024
        ),
    )(pack_rows, segment, planes, norm_gain.reshape(1, columns), out_weight.reshape(2, HALF, columns))


def solution(mesh):
    in_specs = (
        P(("dp", "seq"), None, "tp"),
        P(("dp", "seq")),
        P(("dp", "seq")),
        P("tp"),
        P("seq", "tp"),
    )
    out_specs = P(("dp", "seq"), "tp")
    return jax.shard_map(body, mesh=mesh, in_specs=in_specs, out_specs=out_specs, check_vma=False)
```

time: 73.7 us -> 70.5 us (0.957)
  Pallas kernels: 71.6 us -> 68.4 us
    pallas_call x1, Pallas kernels: 71.6 us -> 68.4 us  [body(): pl.pallas_call(kernel, out_shape=jax.ShapeDtypeStruct((rows, columns), BF...]
where the time goes in v3:
time: 70.5 us; the launch traced here: 70.3 us
  Pallas kernels  68.4 us (97%)
  local copies, waits for them, and re-layouts  1.87 us (3%)
    pallas_call x1, Pallas kernels, body(): pl.pallas_call(kernel, out_shape=jax.ShapeDtypeStruct((rows, columns), BF...  68.4 us
    unnamed x1, local copies, waits for them, and re-layouts  1.87 us

profile of v3, /device:TPU:16, one launch (start us, length us, event | category | flops | bytes accessed | tf_op | source)
XLA Modules:
  0.0 70.3 jit_solution(6903997236291886853)
XLA Ops:
  0.0 68.4 %shard_map.55 = bf16[512,512]{1,0:T(8,128)(2,1)} custom-call(s32[4]{0:T(128)} %pack_hbm.1, s32[4]{0:T(128)} %seg_hbm.1, bf16[3,4,128,512]{3,2,1,0:T(8,128)(2,1)} %bitcast.5, f32[1,512]{1,0:T(1,128)} %bitcast.7, bf16[2,64,512]{2,1,0:T(8,128)(2,1)} %bitcast.6), custom_call_target="tpu_custom_call" | custom-call | tf_op jit(solution)/shard_map/pallas_call | solution.py:276
  68.4 1.9 %copy.7 = bf16[512,512]{1,0:T(8,128)(2,1)} copy(bf16[512,512]{1,0:T(8,128)(2,1)} %shard_map.55) | data formatting | bytes 1048576

commit v4 on v3

--- a/solution.py
+++ b/solution.py
@@ -32,11 +32,11 @@
 
 
 def kernel(
-    pack_hbm, seg_hbm, qkv_hbm, gain_hbm, w_hbm, out_ref,
+    pack_hbm, seg_hbm, qkv_hbm, gain_hbm, w_hbm, out_hbm,
     pack_ref, seg_ref, gain_ref, qbuf, kbuf, vbuf, wbuf, feats, acc, intra, local, tsend, pieces, infos, ascan, rbuf,
-    csend, carry,
-    load_sem, info_s, info_r, t_s, t_r, r_s, r_r, c_s, c_r,
-    y_s, y_r, wx_s, wx_r, wz_s, wz_r, pair_s, pair_r,
+    csend, carry, mixed,
+    load_sem, out_sem, info_s, info_r, t_s, t_r, r_s, r_r, c_s, c_r,
+    y_s, y_r0, y_r, wx_s, wx_r, wz_s, wz_r, pair_s, pair_r,
 ):
     seq, tp, core = lax.axis_index("seq"), lax.axis_index("tp"), lax.axis_index("dp")
     x, z = seq // NZ, seq % NZ
@@ -68,13 +68,13 @@
             (pack_hbm, pack_ref), (seg_hbm, seg_ref), (gain_hbm, gain_ref),
         ))
     ]
-    for i in (5, 4, 1, 2, 0, 3, 6):
-        loads[i].start()
     partners = [at_z(i) for i in (4, 3, 5, 2, 6, 1, 7)] + [at_x(i) for i in (2, 1, 3)]
     partners += [at_y(1), at_y(NY - 1), sibling]
     barrier = pltpu.get_barrier_semaphore()
     for device in partners:
         pl.semaphore_signal(barrier, inc=1, device_id=device, device_id_type=MESH)
+    for i in (5, 4, 1, 2, 0, 3, 6):
+        loads[i].start()
     loads[5].wait()
     loads[4].wait()
     segs = [seg_ref[b] for b in range(NB)]
@@ -113,11 +113,11 @@
     loads[1].wait()
     loads[2].wait()
     update(0)
+    update(1)
     pl.semaphore_wait(barrier, len(partners))
-    send_tails(0)
     for i in far_first:
         remote(infos.at[z], infos.at[z], info_s, info_r, at_z(i)).start()
-    update(1)
+    send_tails(0)
     send_tails(1)
     loads[3].wait()
     for i in (2, 1, 3):
@@ -193,24 +193,35 @@
                 source = (z - 1 - step) % NZ if direction == 0 else (z + 1 + step) % NZ
                 w_pair(w_ref(part, source, core)).start()
 
-    def y_copy(direction, step, g, b):
+    def y_own(direction, g, b):
+        ref = feats.at[tp, g, block_rows(b)]
+        return remote(ref, ref, y_s, y_r0.at[direction, g, b], at_y(1) if direction == 0 else at_y(NY - 1))
+
+    def y_copy(direction, step, b):
         source = (tp - step) % NY if direction == 0 else (tp + step) % NY
-        ref = feats.at[source, g, block_rows(b)]
+        ref = feats.at[source, :, block_rows(b)]
         to = at_y(1) if direction == 0 else at_y(NY - 1)
-        return remote(ref, ref, y_s, y_r.at[direction, step, g, b], to)
-
-    def y_arrive(step, g, b):
+        return remote(ref, ref, y_s, y_r.at[direction, step - 1, b], to)
+
+    def y_arrive(step, i):
         for direction in range(2):
+            b = y_order[direction][i]
             if hops(direction, b) > step:
-                y_copy(direction, step, g, b).wait_recv()
+                if step == 0:
+                    for g in range(NG):
+                        y_own(direction, g, b).wait_recv()
+                else:
+                    y_copy(direction, step, b).wait_recv()
                 if hops(direction, b) > step + 1:
-                    y_copy(direction, step + 1, g, b).start()
-
+                    y_copy(direction, step + 1, b).start()
+
+    y_order = ((0, 1, 2, 3), (2, 3, 0, 1))
+    ready = {0: ((0, 0),), 2: ((1, 2),), 1: ((0, 1), (0, 2)), 3: ((1, 3), (1, 0), (1, 1), (0, 3))}
     loads[6].wait()
     gains = gain_ref[...]
     for g in range(NG):
         wait_all(carry.at[g, pl.ds(0, NZ - 1)], c_r.at[g])
-        for b in range(NB):
+        for b in (0, 2, 1, 3):
             carried = same(segs[b], segs[0])
             for h in range(GH):
                 head = g * GH + h
@@ -222,8 +233,8 @@
                 scale = lax.rsqrt(jnp.mean(attended * attended, axis=-1, keepdims=True) + 1e-06)
                 normed = attended * scale * gains[:, head * DH:(head + 1) * DH]
                 feats[tp, g, block_rows(b), heads[h]] = normed.astype(BF16)
-            for direction in range(2):
-                y_copy(direction, 0, g, b).start()
+            for direction, part in ready[b]:
+                y_own(direction, g, part).start()
 
     def weights(source, g):
         return wbuf[source // 2, pl.ds(source % 2 * NH + g * GH, GH)].reshape(GC, NH * DH)
@@ -233,31 +244,29 @@
         total = dot(feats[source, 0], weights(source, 0)) + dot(feats[source, 1], weights(source, 1))
         acc[...] = total if step == 0 else acc[...] + total
 
-    parts = [(g, b) for g in range(NG) for b in range(NB)]
     w_order = [(step, part) for step in range(4) for part in range(2)]
     for step in range(2):
-        for i, (g, b) in enumerate(parts):
-            y_arrive(step, g, b)
-            if i % 2 == 1:
-                w_arrive(*w_order[step * NB + i // 2])
+        for i in range(NB):
+            y_arrive(step, i)
+            w_arrive(*w_order[step * NB + i])
     wait_all(wbuf.at[:, :, 1 - core], pair_r)
-    for i, (g, b) in enumerate(parts):
-        y_arrive(2, g, b)
-        if i < 5:
-            product((0, 1, NY - 1, 2, NY - 2)[i])
+    for i in range(NB):
+        y_arrive(2, i)
+        product((0, 1, NY - 1, 2)[i])
+    product(NY - 2)
     product(3)
     product(NY - 3)
 
     far = (tp + NY // 2) % NY
-    for g in range(NG):
-        for b in (0, NB // 2, 1, NB // 2 + 1):
-            y_arrive(3, g, b)
+    for i in range(NB // 2):
+        y_arrive(3, i)
+        for b in (i, i + NB // 2):
             rows = block_rows(b)
-            total = acc[rows, :] + dot(feats[far, g, rows, :], weights(far, g))
-            if g < NG - 1:
-                acc[rows, :] = total
-            else:
-                out_ref[rows, :] = total.astype(BF16)
+            total = acc[rows, :]
+            for g in range(NG):
+                total = total + dot(feats[far, g, rows, :], weights(far, g))
+            mixed[rows, :] = total.astype(BF16)
+            pltpu.make_async_copy(mixed.at[rows], out_hbm.at[rows], out_sem).start()
 
     wait_all(infos.at[pl.ds(0, NZ - 1)], info_s)
     wait_all(pieces.at[:, pl.ds(0, NZ - 1)], t_s)
@@ -267,6 +276,7 @@
     wait_all(wbuf.at[:, pl.ds(0, NZ - 1), core], wz_s)
     wait_all(wbuf.at[:, :, core], pair_s)
     wait_all(feats.at[pl.ds(0, NY - 1)], y_s)
+    wait_all(mixed, out_sem)
 
 
 def body(qkv_bank, pack_rows, segment, norm_gain, out_weight):
@@ -277,7 +287,7 @@
         kernel,
         out_shape=jax.ShapeDtypeStruct((rows, columns), BF16),
         in_specs=[pl.BlockSpec(memory_space=pl.ANY)] * 5,
-        out_specs=pl.BlockSpec(memory_space=pltpu.VMEM),
+        out_specs=pl.BlockSpec(memory_space=pl.ANY),
         scratch_shapes=[
             pltpu.SMEM((NB,), jnp.int32),
             pltpu.SMEM((NB,), jnp.int32),
@@ -297,8 +307,9 @@
             pltpu.VMEM((NG, NX, PIECE + 8, DH), F32),
             pltpu.VMEM((NG, NZ, PIECE, DH), BF16),
             pltpu.VMEM((NG, NZ, PIECE, DH), BF16),
-            dma((7,)), dma, dma, dma, dma((NG,)), dma, dma((NG,)), dma, dma((NG,)),
-            dma, dma((2, 4, NG, NB)), dma, dma, dma, dma((2, 4, 2)), dma, dma,
+            pltpu.VMEM((rows, columns), BF16),
+            dma((7,)), dma, dma, dma, dma, dma((NG,)), dma, dma((NG,)), dma, dma((NG,)),
+            dma, dma((2, NG, NB)), dma((2, 3, NB)), dma, dma, dma, dma((2, 4, 2)), dma, dma,
         ],
         compiler_params=pltpu.CompilerParams(
             collective_id=0, has_side_effects=True, vmem_limit_bytes=60 * 1024 * 1024

time: 70.5 us -> 69.2 us (0.982)
  the two profiles are of different devices: /device:TPU:16 before, /device:TPU:6 now
where the time goes in v4:
time: 69.2 us; the launch traced here: 67.8 us
  Pallas kernels  65.9 us (95%)
  local copies, waits for them, and re-layouts  1.87 us (3%)
    pallas_call x1, Pallas kernels, body(): pl.pallas_call(kernel, out_shape=jax.ShapeDtypeStruct((rows, columns), BF...  65.9 us
    unnamed x1, local copies, waits for them, and re-layouts  1.87 us

profile of v4, /device:TPU:6, one launch (start us, length us, event | category | flops | bytes accessed | tf_op | source)
XLA Modules:
  0.0 67.8 jit_solution(3746062976677534921)
XLA Ops:
  0.0 65.9 %shard_map.55 = bf16[512,512]{1,0:T(8,128)(2,1)} custom-call(s32[4]{0:T(128)} %pack_hbm.1, s32[4]{0:T(128)} %seg_hbm.1, bf16[3,4,128,512]{3,2,1,0:T(8,128)(2,1)} %bitcast.5, f32[1,512]{1,0:T(1,128)} %bitcast.7, bf16[2,64,512]{2,1,0:T(8,128)(2,1)} %bitcast.6), custom_call_target="tpu_custom_call" | custom-call | tf_op jit(solution)/shard_map/pallas_call | solution.py:286
  65.9 1.9 %copy.7 = bf16[512,512]{1,0:T(8,128)(2,1)} copy(bf16[512,512]{1,0:T(8,128)(2,1)} %shard_map.55) | data formatting | bytes 1048576

commit v5 on v4

--- a/solution.py
+++ b/solution.py
@@ -36,7 +36,7 @@
     pack_ref, seg_ref, gain_ref, qbuf, kbuf, vbuf, wbuf, feats, acc, intra, local, tsend, pieces, infos, ascan, rbuf,
     csend, carry, mixed,
     load_sem, out_sem, info_s, info_r, t_s, t_r, r_s, r_r, c_s, c_r,
-    y_s, y_r0, y_r, wx_s, wx_r, wz_s, wz_r, pair_s, pair_r,
+    y_s, y_r, wx_s, wx_r, wz_s, wz_r, pair_s, pair_r,
 ):
     seq, tp, core = lax.axis_index("seq"), lax.axis_index("tp"), lax.axis_index("dp")
     x, z = seq // NZ, seq % NZ
@@ -129,7 +129,7 @@
     def block_rows(b):
         return pl.ds(b * BLK, BLK)
 
-    for h in range(NH):
+    def scores(h):
         for b in range(NB):
             query = qbuf[ids[b], :, heads[h]]
             key = kbuf[ids[b], :, heads[h]]
@@ -137,6 +137,9 @@
             score = dot(query, key, (((1,), (1,)), ((), ())))
             score = jnp.where(causal, score, 0.0).astype(BF16)
             intra[block_rows(b), heads[h]] = dot(score, value)
+
+    scores(0)
+    scores(1)
 
     wait_all(infos.at[pl.ds(0, NZ - 1)], info_r)
     firsts = [infos[j, 0:1, :] for j in range(NZ)]
@@ -146,25 +149,31 @@
     for g in range(NG):
         wait_all(pieces.at[g, pl.ds(0, NZ - 1)], t_r.at[g])
         running = pieces[g, 0].astype(F32)
+        ascan[g, 0] = jnp.zeros((PIECE, DH), F32)
         for j in range(1, NZ):
             before = follows[j] * running
             ascan[g, j] = before
             running = pieces[g, j].astype(F32) + stays[j] * before
         rbuf[g, x, 0:PIECE, :] = running
         rbuf[g, x, PIECE:PIECE + 8, :] = jnp.broadcast_to(lasts[NZ - 1], (8, DH))
-        for i in (2, 1, 3):
+        for i in (2, 1):
             remote(rbuf.at[g, x], rbuf.at[g, x], r_s, r_r.at[g], at_x(i)).start()
+    scores(2)
     for g in range(NG):
-        wait_all(rbuf.at[g, pl.ds(0, NX - 1)], r_r.at[g])
-        for j in range(NZ):
-            into = ascan[g, j] if j > 0 else jnp.zeros((PIECE, DH), F32)
-            for xx in range(NX - 1):
-                hit = same(rbuf[g, xx, PIECE:PIECE + 1, :], firsts[j]) * jnp.where(xx < x, 1.0, 0.0)
+        wait_all(rbuf.at[g, pl.ds(0, 2)], r_r.at[g])
+        for i in far_first + (0,):
+            j = (z + i) % NZ
+            into = ascan[g, j]
+            for back in (1, 2):
+                xx = (x + NX - back) % NX
+                hit = same(rbuf[g, xx, PIECE:PIECE + 1, :], infos[j, 0:1, :]) * jnp.where(x >= back, 1.0, 0.0)
                 into = into + hit * rbuf[g, xx, 0:PIECE, :]
             csend[g, j] = into.astype(BF16)
-        for i in far_first:
-            remote(csend.at[g, (z + i) % NZ], carry.at[g, z], c_s, c_r.at[g], at_z(i)).start()
+            if i > 0:
+                remote(csend.at[g, j], carry.at[g, z], c_s, c_r.at[g], at_z(i)).start()
         carry[g, z] = csend[g, z]
+
+    scores(3)
 
     def w_ref(part, column, side):
         return wbuf.at[pl.ds(2 * part, 2), column, side]
@@ -195,33 +204,29 @@
 
     def y_own(direction, g, b):
         ref = feats.at[tp, g, block_rows(b)]
-        return remote(ref, ref, y_s, y_r0.at[direction, g, b], at_y(1) if direction == 0 else at_y(NY - 1))
+        return remote(ref, ref, y_s, y_r.at[direction, 0, b], at_y(1) if direction == 0 else at_y(NY - 1))
 
     def y_copy(direction, step, b):
         source = (tp - step) % NY if direction == 0 else (tp + step) % NY
         ref = feats.at[source, :, block_rows(b)]
         to = at_y(1) if direction == 0 else at_y(NY - 1)
-        return remote(ref, ref, y_s, y_r.at[direction, step - 1, b], to)
+        return remote(ref, ref, y_s, y_r.at[direction, step, b], to)
 
     def y_arrive(step, i):
         for direction in range(2):
             b = y_order[direction][i]
             if hops(direction, b) > step:
-                if step == 0:
-                    for g in range(NG):
-                        y_own(direction, g, b).wait_recv()
-                else:
-                    y_copy(direction, step, b).wait_recv()
+                y_copy(direction, step, b).wait_recv()
                 if hops(direction, b) > step + 1:
                     y_copy(direction, step + 1, b).start()
 
     y_order = ((0, 1, 2, 3), (2, 3, 0, 1))
-    ready = {0: ((0, 0),), 2: ((1, 2),), 1: ((0, 1), (0, 2)), 3: ((1, 3), (1, 0), (1, 1), (0, 3))}
+    ready = {b: ((0, b), (1, b)) for b in range(NB)}
     loads[6].wait()
     gains = gain_ref[...]
     for g in range(NG):
         wait_all(carry.at[g, pl.ds(0, NZ - 1)], c_r.at[g])
-        for b in (0, 2, 1, 3):
+        for b in (0, 1, 2, 3):
             carried = same(segs[b], segs[0])
             for h in range(GH):
                 head = g * GH + h
@@ -270,7 +275,7 @@
 
     wait_all(infos.at[pl.ds(0, NZ - 1)], info_s)
     wait_all(pieces.at[:, pl.ds(0, NZ - 1)], t_s)
-    wait_all(rbuf.at[:, pl.ds(0, NX - 1)], r_s)
+    wait_all(rbuf.at[:, pl.ds(0, 2)], r_s)
     wait_all(carry.at[:, pl.ds(0, NZ - 1)], c_s)
     wait_all(wbuf.at[pl.ds(0, NX - 1), z, core], wx_s)
     wait_all(wbuf.at[:, pl.ds(0, NZ - 1), core], wz_s)
@@ -309,7 +314,7 @@
             pltpu.VMEM((NG, NZ, PIECE, DH), BF16),
             pltpu.VMEM((rows, columns), BF16),
             dma((7,)), dma, dma, dma, dma, dma((NG,)), dma, dma((NG,)), dma, dma((NG,)),
-            dma, dma((2, NG, NB)), dma((2, 3, NB)), dma, dma, dma, dma((2, 4, 2)), dma, dma,
+            dma, dma((2, 4, NB)), dma, dma, dma, dma((2, 4, 2)), dma, dma,
         ],
         compiler_params=pltpu.CompilerParams(
             collective_id=0, has_side_effects=True, vmem_limit_bytes=60 * 1024 * 1024

time: 69.2 us -> 68.8 us (level)
  no operation moved by 1% of the time
where the time goes in v5:
time: 68.8 us; the launch traced here: 67.7 us
  Pallas kernels  65.8 us (96%)
  local copies, waits for them, and re-layouts  1.87 us (3%)
    pallas_call x1, Pallas kernels, body(): pl.pallas_call(kernel, out_shape=jax.ShapeDtypeStruct((rows, columns), BF...  65.8 us
    unnamed x1, local copies, waits for them, and re-layouts  1.87 us

profile of v5, /device:TPU:6, one launch (start us, length us, event | category | flops | bytes accessed | tf_op | source)
XLA Modules:
  0.0 67.7 jit_solution(7815691056920285026)
XLA Ops:
  0.0 65.8 %shard_map.55 = bf16[512,512]{1,0:T(8,128)(2,1)} custom-call(s32[4]{0:T(128)} %pack_hbm.1, s32[4]{0:T(128)} %seg_hbm.1, bf16[3,4,128,512]{3,2,1,0:T(8,128)(2,1)} %bitcast.5, f32[1,512]{1,0:T(1,128)} %bitcast.7, bf16[2,64,512]{2,1,0:T(8,128)(2,1)} %bitcast.6), custom_call_target="tpu_custom_call" | custom-call | tf_op jit(solution)/shard_map/pallas_call | solution.py:291
  65.8 1.9 %copy.7 = bf16[512,512]{1,0:T(8,128)(2,1)} copy(bf16[512,512]{1,0:T(8,128)(2,1)} %shard_map.55) | data formatting | bytes 1048576

commit v6 on v5

--- a/solution.py
+++ b/solution.py
@@ -154,20 +154,23 @@
             before = follows[j] * running
             ascan[g, j] = before
             running = pieces[g, j].astype(F32) + stays[j] * before
-        rbuf[g, x, 0:PIECE, :] = running
-        rbuf[g, x, PIECE:PIECE + 8, :] = jnp.broadcast_to(lasts[NZ - 1], (8, DH))
+        rbuf[g, x, 0:PIECE, :] = running.astype(BF16)
+        rbuf[g, x, PIECE:PIECE + 16, :] = jnp.broadcast_to(lasts[NZ - 1], (16, DH)).astype(BF16)
         for i in (2, 1):
             remote(rbuf.at[g, x], rbuf.at[g, x], r_s, r_r.at[g], at_x(i)).start()
     scores(2)
     for g in range(NG):
         wait_all(rbuf.at[g, pl.ds(0, 2)], r_r.at[g])
+        earlier = []
+        for back in (1, 2):
+            xx = (x + NX - back) % NX
+            total = rbuf[g, xx, 0:PIECE, :].astype(F32) * jnp.where(x >= back, 1.0, 0.0)
+            earlier.append((total, rbuf[g, xx, PIECE:PIECE + 16, :].astype(F32)[0:1]))
         for i in far_first + (0,):
             j = (z + i) % NZ
             into = ascan[g, j]
-            for back in (1, 2):
-                xx = (x + NX - back) % NX
-                hit = same(rbuf[g, xx, PIECE:PIECE + 1, :], infos[j, 0:1, :]) * jnp.where(x >= back, 1.0, 0.0)
-                into = into + hit * rbuf[g, xx, 0:PIECE, :]
+            for total, last in earlier:
+                into = into + same(last, infos[j, 0:1, :]) * total
             csend[g, j] = into.astype(BF16)
             if i > 0:
                 remote(csend.at[g, j], carry.at[g, z], c_s, c_r.at[g], at_z(i)).start()
@@ -309,7 +312,7 @@
             pltpu.VMEM((NG, NZ, PIECE, DH), BF16),
             pltpu.VMEM((NZ, 2, DH), F32),
             pltpu.VMEM((NG, NZ, PIECE, DH), F32),
-            pltpu.VMEM((NG, NX, PIECE + 8, DH), F32),
+            pltpu.VMEM((NG, NX, PIECE + 16, DH), BF16),
             pltpu.VMEM((NG, NZ, PIECE, DH), BF16),
             pltpu.VMEM((NG, NZ, PIECE, DH), BF16),
             pltpu.VMEM((rows, columns), BF16),

time: 68.8 us -> 68.7 us (level)
  no operation moved by 1% of the time
where the time goes in v6:
time: 68.7 us; the launch traced here: 67.6 us
  Pallas kernels  65.7 us (96%)
  local copies, waits for them, and re-layouts  1.87 us (3%)
    pallas_call x1, Pallas kernels, body(): pl.pallas_call(kernel, out_shape=jax.ShapeDtypeStruct((rows, columns), BF...  65.7 us
    unnamed x1, local copies, waits for them, and re-layouts  1.87 us

profile of v6, /device:TPU:6, one launch (start us, length us, event | category | flops | bytes accessed | tf_op | source)
XLA Modules:
  0.0 67.6 jit_solution(1883067851390168028)
XLA Ops:
  0.0 65.7 %shard_map.55 = bf16[512,512]{1,0:T(8,128)(2,1)} custom-call(s32[4]{0:T(128)} %pack_hbm.1, s32[4]{0:T(128)} %seg_hbm.1, bf16[3,4,128,512]{3,2,1,0:T(8,128)(2,1)} %bitcast.5, f32[1,512]{1,0:T(1,128)} %bitcast.7, bf16[2,64,512]{2,1,0:T(8,128)(2,1)} %bitcast.6), custom_call_target="tpu_custom_call" | custom-call | tf_op jit(solution)/shard_map/pallas_call | solution.py:294
  65.8 1.9 %copy.7 = bf16[512,512]{1,0:T(8,128)(2,1)} copy(bf16[512,512]{1,0:T(8,128)(2,1)} %shard_map.55) | data formatting | bytes 1048576

commit v7 on v6

--- a/solution.py
+++ b/solution.py
@@ -157,13 +157,14 @@
         rbuf[g, x, 0:PIECE, :] = running.astype(BF16)
         rbuf[g, x, PIECE:PIECE + 16, :] = jnp.broadcast_to(lasts[NZ - 1], (16, DH)).astype(BF16)
         for i in (2, 1):
-            remote(rbuf.at[g, x], rbuf.at[g, x], r_s, r_r.at[g], at_x(i)).start()
+            pl.when(x + i < NX)(remote(rbuf.at[g, x], rbuf.at[g, x], r_s, r_r.at[g], at_x(i)).start)
     scores(2)
     for g in range(NG):
-        wait_all(rbuf.at[g, pl.ds(0, 2)], r_r.at[g])
+        for count, here in ((1, x == 1), (2, x >= 2)):
+            pl.when(here)(lambda: wait_all(rbuf.at[g, pl.ds(0, count)], r_r.at[g]))
         earlier = []
         for back in (1, 2):
-            xx = (x + NX - back) % NX
+            xx = jnp.where(x >= back, x - back, x)
             total = rbuf[g, xx, 0:PIECE, :].astype(F32) * jnp.where(x >= back, 1.0, 0.0)
             earlier.append((total, rbuf[g, xx, PIECE:PIECE + 16, :].astype(F32)[0:1]))
         for i in far_first + (0,):
@@ -278,7 +279,8 @@
 
     wait_all(infos.at[pl.ds(0, NZ - 1)], info_s)
     wait_all(pieces.at[:, pl.ds(0, NZ - 1)], t_s)
-    wait_all(rbuf.at[:, pl.ds(0, 2)], r_s)
+    for count, here in ((2, x < NX - 2), (1, x == NX - 2)):
+        pl.when(here)(lambda: wait_all(rbuf.at[:, pl.ds(0, count)], r_s))
     wait_all(carry.at[:, pl.ds(0, NZ - 1)], c_s)
     wait_all(wbuf.at[pl.ds(0, NX - 1), z, core], wx_s)
     wait_all(wbuf.at[:, pl.ds(0, NZ - 1), core], wz_s)

time: 68.7 us -> 67.8 us (0.987); the launches traced: 67.6 us -> 67.6 us
  no operation moved by 1% of the time
where the time goes in v7:
time: 67.8 us; the launch traced here: 67.6 us
  Pallas kernels  65.7 us (97%)
  local copies, waits for them, and re-layouts  1.87 us (3%)
    pallas_call x1, Pallas kernels, body(): pl.pallas_call(kernel, out_shape=jax.ShapeDtypeStruct((rows, columns), BF...  65.7 us
    unnamed x1, local copies, waits for them, and re-layouts  1.87 us

profile of v7, /device:TPU:6, one launch (start us, length us, event | category | flops | bytes accessed | tf_op | source)
XLA Modules:
  0.0 67.6 jit_solution(9580982228092338089)
XLA Ops:
  0.0 65.7 %shard_map.55 = bf16[512,512]{1,0:T(8,128)(2,1)} custom-call(s32[4]{0:T(128)} %pack_hbm.1, s32[4]{0:T(128)} %seg_hbm.1, bf16[3,4,128,512]{3,2,1,0:T(8,128)(2,1)} %bitcast.5, f32[1,512]{1,0:T(1,128)} %bitcast.7, bf16[2,64,512]{2,1,0:T(8,128)(2,1)} %bitcast.6), custom_call_target="tpu_custom_call" | custom-call | tf_op jit(solution)/shard_map/pallas_call | solution.py:296
  65.8 1.9 %copy.7 = bf16[512,512]{1,0:T(8,128)(2,1)} copy(bf16[512,512]{1,0:T(8,128)(2,1)} %shard_map.55) | data formatting | bytes 1048576
